TPU v7x, 32 devices: a whole 2x2x4 slice. The times are simulated.
32 devices in a mesh: seq: 16 (over z, x, core), wshard: 2 (over y).
Axes of the slice: x: 2, y: 2, z: 4, core: 2. Of those that a mesh axis runs over, the one named last changes fastest.
Arguments:
- hidden: bfloat16 [8, 2048, 1024], P('wshard', 'seq'), may hold values from -6 to 6
- segments: int32 [8, 2048], P('wshard', 'seq'), may hold values from 0 to 2, never falling along the last dimension, each value on 1 to 1536 neighbouring positions
- cotangent: bfloat16 [8, 2048, 1024], P('wshard', 'seq'), may hold values from -6 to 6
- in_weight: bfloat16 [1024, 3, 1024], P(None, None, 'wshard'), may hold values from -0.1875 to 0.1875
- out_weight: bfloat16 [1024, 1024], P('wshard'), may hold values from -0.1875 to 0.1875
- gate_weight: bfloat16 [1024, 4608], P(None, 'wshard'), may hold values from -0.1875 to 0.1875
- up_weight: bfloat16 [1024, 4608], P(None, 'wshard'), may hold values from -0.1875 to 0.1875
- down_weight: bfloat16 [4608, 1024], P('wshard'), may hold values from -0.09375 to 0.09375
- conv_weight: bfloat16 [3, 1024], P(None, 'wshard'), may hold values from -3 to 3
- norm_mix: bfloat16 [1024], P('wshard'), may hold values from 0.5 to 1.5
- norm_ffn: bfloat16 [1024], P('wshard'), may hold values from 0.5 to 1.5
Outputs:
- block_out: bfloat16 [8, 2048, 1024], P('wshard', 'seq')
- grad_hidden: float32 [8, 2048, 1024], P('wshard', 'seq')
- grad_in: float32 [1024, 3, 1024], P('seq', None, 'wshard')
- grad_out: float32 [1024, 1024], P('wshard', 'seq')
- grad_gate: float32 [1024, 4608], P('seq', 'wshard')
- grad_up: float32 [1024, 4608], P('seq', 'wshard')
- grad_down: float32 [4608, 1024], P('wshard', 'seq')
- grad_conv: float32 [3, 1024], P(None, 'wshard')
- grad_norm_mix: float32 [1024], P('wshard')
- grad_norm_ffn: float32 [1024], P('wshard')
Inputs may be any that keep to these rules, and one draw needn't show every extreme that they name: `segments`: segment numbers never fall along a sequence; each document holds 1 to 1536 tokens, one exactly that many.
All inputs are finite; a program needn't handle non-finite values.
Results may differ from a plain program's by a relative error of at most 0.017.
Values may be sent and summed in bfloat16 or wider, within the bound.
No kernel may reach another device: no remote copies, remote signals or barrier semaphores. Data moves between devices by JAX's collectives and lax.ppermute only.
A program may use at most 256 MiB of HBM per device.

v0:
```python
import jax
import jax.numpy as jnp
from jax import lax
from jax.sharding import PartitionSpec as P

EPS = 1e-05
LOW = jnp.bfloat16
F32 = jnp.float32


def over_seq(block, route):
    return lax.ppermute(block, "seq", route)


def swap_seq(block, mask):
    return over_seq(block, [(i, i ^ mask) for i in range(lax.axis_size("seq"))])


def swap_core(block):
    return swap_seq(block, 1)


def swap_pair(block):
    return lax.ppermute(block, "wshard", [(0, 1), (1, 0)])


def swap(block, link):
    return swap_pair(block) if link == "pair" else swap_seq(block, 2 * link)


def mm(left, right):
    return jnp.dot(left, right, preferred_element_type=F32)


def mm_tn(left, right):
    return lax.dot_general(left, right, (((0,), (0,)), ((), ())), preferred_element_type=F32)


def mm_nt(left, right):
    return lax.dot_general(left, right, (((1,), (1,)), ((), ())), preferred_element_type=F32)


def norm_stats(values):
    return lax.rsqrt(jnp.mean(values * values, axis=-1, keepdims=True) + EPS)


def norm_back(upstream, values, scale, gain):
    scaled = values * scale
    weighted = upstream * gain
    inner = jnp.mean(weighted * scaled, axis=-1, keepdims=True)
    return scale * (weighted - scaled * inner)


def slot_masks(order):
    masks = [0]
    for link in reversed(order):
        masks = masks + [mask ^ link for mask in masks]
    return masks


def in_slots(grad, chip, order):
    chips = lax.axis_size("seq") // 2
    blocks = grad.astype(LOW).reshape(chips, grad.shape[0] // chips, grad.shape[1])
    return jnp.stack(
        [lax.dynamic_index_in_dim(blocks, chip ^ mask, 0, False) for mask in slot_masks(order)]
    )


def halving(send, keep, order):
    terms = [keep]
    half = keep.shape[0]
    terms.append(swap(send, order[0]))
    for link in order[1:]:
        half //= 2
        going = sum((term[half : 2 * half].astype(F32) for term in terms)).astype(LOW)
        terms.append(swap(going, link))
    return sum((term[0].astype(F32) for term in terms))


def scatter_seq(grad, chip, order):
    slots = in_slots(grad, chip, order)
    half = slots.shape[0] // 2
    return halving(slots[half:], slots[:half], order)


def scatter_all(mine, other, chip, order):
    return halving(in_slots(other, chip, order[1:]), in_slots(mine, chip, order[1:]), order)


def local(
    hidden,
    segments,
    cotangent,
    in_weight,
    out_weight,
    gate_weight,
    up_weight,
    down_weight,
    conv_weight,
    norm_mix,
    norm_ffn,
):
    groups, block, width = hidden.shape
    rows = groups * block
    size = lax.axis_size("seq")
    seq_index = lax.axis_index("seq")
    core = seq_index % 2
    chip = seq_index // 2
    pair = lax.axis_index("wshard")
    first_core = core == 0
    chips = size // 2
    links = [1 << bit for bit in range(chips.bit_length() - 1)]
    features = out_weight.shape[0] // 2
    units = gate_weight.shape[1] // 2

    def ordered(flag, mine, other, axis):
        return jnp.where(
            flag,
            jnp.concatenate([mine, other], axis=axis),
            jnp.concatenate([other, mine], axis=axis),
        )

    small = jnp.concatenate([conv_weight, norm_mix[None], norm_ffn[None]], axis=0)
    small_other = swap_pair(small)
    gains = ordered(pair == 0, small[3:], small_other[3:], 1).astype(F32)
    gain_mix, gain_ffn = (gains[0], gains[1])

    def of_core(array, axis):
        return lax.dynamic_slice_in_dim(
            array, core * (array.shape[axis] // 2), array.shape[axis] // 2, axis
        )

    taps = jnp.concatenate([of_core(small[:3], 1), of_core(small_other[:3], 1)], axis=1).astype(F32)
    in_mine = of_core(jnp.transpose(in_weight, (1, 0, 2)), 2)
    in_other = swap_pair(in_mine)
    out_mine = of_core(out_weight, 0)
    out_other = swap_pair(out_mine)
    in_mat = jnp.concatenate([part for j in range(3) for part in (in_mine[j], in_other[j])], axis=1)
    out_mat = jnp.concatenate([out_mine, out_other], axis=0)
    conv_width = 2 * features
    own = hidden.reshape(rows, width)
    chip_hidden = jnp.concatenate([own, swap_core(own)], axis=0)
    seg_low = segments.astype(LOW)
    seg_other = swap_core(segments)
    edge = jnp.concatenate(
        [hidden, jnp.broadcast_to(seg_low[:, :, None], (groups, block, 128))], axis=2
    )
    last, head = (edge[:, block - 2 :], edge[:, :2])
    odd = range(1, size - 1, 2)
    even = range(2, size, 2)
    before = jnp.where(
        first_core,
        over_seq(last, [(i, i + 1) for i in odd]),
        over_seq(last, [(i, i + 2) for i in odd]),
    )
    after = jnp.where(
        first_core,
        over_seq(head, [(i, i - 2) for i in even]),
        over_seq(head, [(i, i - 1) for i in even]),
    )
    edges = jnp.concatenate([before, after], axis=0)
    edge_hidden = edges[:, :, :width].reshape(4 * groups, width)
    edge_segs = edges[:, :, width].astype(jnp.int32)
    resid = chip_hidden.astype(F32)
    scale_mix = norm_stats(resid)
    normed_mix = (resid * scale_mix * gain_mix).astype(LOW)
    edge_resid = edge_hidden.astype(F32)
    edge_normed = (edge_resid * norm_stats(edge_resid) * gain_mix).astype(LOW)
    projected = mm(normed_mix, in_mat)
    edge_projected = mm(edge_normed, in_mat)
    b_part = projected[:, :conv_width]
    c_part = projected[:, conv_width : 2 * conv_width]
    x_part = projected[:, 2 * conv_width :]

    def by_core(array):
        return array.reshape((2, groups, block) + array.shape[1:])

    def lead(own_lead, other_lead):
        return jnp.stack([own_lead, other_lead])

    conv_in = by_core((b_part * x_part).astype(LOW).astype(F32))
    edge_conv_in = (
        (edge_projected[: 2 * groups, :conv_width] * edge_projected[: 2 * groups, 2 * conv_width :])
        .astype(LOW)
        .astype(F32)
        .reshape(groups, 2, conv_width)
    )
    edge_c = edge_projected[2 * groups :, conv_width : 2 * conv_width]
    segs = jnp.stack([segments, seg_other])
    segs_before, segs_after = (edge_segs[:groups], edge_segs[groups:])

    def with_before(values, outside):
        ahead = jnp.where(
            first_core,
            lead(outside, values[0, :, block - 2 :]),
            lead(values[1, :, block - 2 :], outside),
        )
        return jnp.concatenate([ahead, values], axis=2)

    def with_after(values, outside):
        behind = jnp.where(
            first_core, lead(values[1, :, :2], outside), lead(outside, values[0, :, :2])
        )
        return jnp.concatenate([values, behind], axis=2)

    ext = with_before(conv_in, edge_conv_in)
    segs_ext = with_before(segs, segs_before)
    keep_one = (segs_ext[:, :, 1 : 1 + block] == segs).astype(F32)[..., None]
    keep_two = (segs_ext[:, :, :block] == segs).astype(F32)[..., None]
    lag_one = keep_one * ext[:, :, 1 : 1 + block]
    lag_two = keep_two * ext[:, :, :block]
    conv_out = (taps[2] * conv_in + taps[1] * lag_one + taps[0] * lag_two).reshape(
        2 * rows, conv_width
    )
    mixed = (c_part * conv_out).astype(LOW)
    mix_part = mm(mixed, out_mat).astype(LOW)
    mix_other = swap_core(mix_part)
    mix_term = mix_part.astype(F32) + jnp.concatenate(
        [mix_other[rows:], mix_other[:rows]], axis=0
    ).astype(F32)
    resid_two = resid + mix_term
    scale_ffn = norm_stats(resid_two)
    normed_ffn = (resid_two * scale_ffn * gain_ffn).astype(LOW)

    def gathered(mine):
        far = swap_pair(mine)
        return (far, swap_core(far))

    cot = cotangent.reshape(rows, width)
    cot_chip = jnp.concatenate([cot, swap_core(cot)], axis=0)
    cot_far = jnp.concatenate(gathered(cot), axis=0)
    normed_far = jnp.concatenate(gathered(normed_ffn[:rows]), axis=0)
    gate_mat = of_core(gate_weight, 1)
    up_mat = of_core(up_weight, 1)
    down_mat = of_core(down_weight, 0)

    def feed_forward(normed, upstream):
        gate = mm(normed, gate_mat)
        up_value = mm(normed, up_mat)
        d_act = mm_nt(upstream, down_mat)
        sigma = jax.nn.sigmoid(gate)
        silu_gate = gate * sigma
        act = (silu_gate * up_value).astype(LOW)
        d_gate = (d_act * up_value * sigma * (1.0 + gate * (1.0 - sigma))).astype(LOW)
        d_up = (d_act * silu_gate).astype(LOW)
        term = mm(act, down_mat).astype(LOW)
        d_normed = (mm_nt(d_gate, gate_mat) + mm_nt(d_up, up_mat)).astype(LOW)
        return (act, d_gate, d_up, term, d_normed)

    near_out = feed_forward(normed_ffn, cot_chip)
    far_out = feed_forward(normed_far, cot_far)

    def home(near, far):
        near_sum = near[:rows].astype(F32) + swap_core(near[rows:]).astype(F32)
        far_sum = (far[:rows].astype(F32) + swap_core(far[rows:]).astype(F32)).astype(LOW)
        return near_sum + swap_pair(far_sum).astype(F32)

    d_normed_ffn = home(near_out[4], far_out[4])
    block_out = (resid_two[:rows] + home(near_out[3], far_out[3])).astype(LOW)
    all_normed = jnp.concatenate([normed_ffn, normed_far], axis=0)
    all_cot = jnp.concatenate([cot_chip, cot_far], axis=0)
    act, d_gate, d_up = (jnp.concatenate([near_out[i], far_out[i]], axis=0) for i in range(3))
    part_down = scatter_seq(mm_tn(all_cot, act), chip, links)
    part_gate = scatter_seq(mm_tn(all_normed, d_gate), chip, links)
    part_up = scatter_seq(mm_tn(all_normed, d_up), chip, links)
    upstream = cot.astype(F32)
    own_two, own_scale = (resid_two[:rows], scale_ffn[:rows])
    d_resid_two = upstream + norm_back(d_normed_ffn, own_two, own_scale, gain_ffn)
    grad_gain_ffn = jnp.sum(d_normed_ffn * own_two * own_scale, axis=0)
    d_resid_low = d_resid_two.astype(LOW)
    d_chip = jnp.concatenate([d_resid_low, swap_core(d_resid_low)], axis=0)
    d_head = d_resid_low.reshape(groups, block, width)[:, :2]
    d_after = jnp.where(
        first_core,
        over_seq(d_head, [(i, i - 2) for i in even]),
        over_seq(d_head, [(i, i - 1) for i in even]),
    ).reshape(2 * groups, width)
    d_mixed = mm_nt(d_chip, out_mat)
    edge_d_conv = (mm_nt(d_after, out_mat) * edge_c).reshape(groups, 2, conv_width)
    d_conv = by_core(d_mixed * c_part)
    d_c = d_mixed * conv_out
    grad_taps = jnp.stack(
        [
            jnp.sum(d_conv * lag_two, axis=(0, 1, 2)),
            jnp.sum(d_conv * lag_one, axis=(0, 1, 2)),
            jnp.sum(d_conv * conv_in, axis=(0, 1, 2)),
        ]
    )
    d_ext = with_after(d_conv, edge_d_conv)
    segs_next = with_after(segs, segs_after)
    next_one = (segs_next[:, :, 1 : 1 + block] == segs).astype(F32)[..., None]
    next_two = (segs_next[:, :, 2 : 2 + block] == segs).astype(F32)[..., None]
    d_conv_in = (
        taps[2] * d_conv
        + taps[1] * next_one * d_ext[:, :, 1 : 1 + block]
        + taps[0] * next_two * d_ext[:, :, 2 : 2 + block]
    ).reshape(2 * rows, conv_width)
    d_proj = jnp.concatenate([d_conv_in * x_part, d_c, d_conv_in * b_part], axis=1).astype(LOW)
    grad_out = mm_tn(d_chip, mixed)
    grad_in = mm_tn(normed_mix, d_proj)
    d_normed_part = mm_nt(d_proj, in_mat).astype(LOW)
    d_normed_mix = d_normed_part[:rows].astype(F32) + swap_core(d_normed_part[rows:]).astype(F32)
    own_resid, own_mix = (resid[:rows], scale_mix[:rows])
    grad_hidden = (d_resid_two + norm_back(d_normed_mix, own_resid, own_mix, gain_mix)).reshape(
        groups, block, width
    )
    grad_gain_mix = jnp.sum(d_normed_mix * own_resid * own_mix, axis=0)
    halves = [grad_out] + [grad_in[:, j * conv_width : (j + 1) * conv_width] for j in range(3)]
    mixed_mine = jnp.concatenate([half[:, :features] for half in halves], axis=1)
    mixed_far = jnp.concatenate([half[:, features:] for half in halves], axis=1)
    part_mix = scatter_all(mixed_mine, mixed_far, chip, ["pair"] + links)
    part_rows = width // size

    def finish(part):
        low = part.astype(LOW).reshape(2, part_rows, -1)
        came = swap_core(lax.dynamic_index_in_dim(low, 1 - core, 0, False)).astype(F32)
        mine = lax.dynamic_index_in_dim(part.reshape(2, part_rows, -1), core, 0, False)
        return (mine, came)

    def wide(part):
        mine, came = finish(part)
        return ordered(first_core, mine, came, 1)

    out_down = wide(part_down).T
    out_gate = wide(part_gate)
    out_up = wide(part_up)
    mix_mine, mix_came = finish(part_mix)
    mix_parts = [
        ordered(
            first_core,
            mix_mine[:, j * features : (j + 1) * features],
            mix_came[:, j * features : (j + 1) * features],
            1,
        )
        for j in range(4)
    ]
    out_out = mix_parts[0].T
    out_in = jnp.stack(mix_parts[1:], axis=1)
    half_width = norm_mix.shape[0]
    spread = jnp.zeros((3, width), F32)
    spread = lax.dynamic_update_slice_in_dim(
        spread, grad_taps[:, :features], pair * half_width + core * features, 1
    )
    spread = lax.dynamic_update_slice_in_dim(
        spread, grad_taps[:, features:], (1 - pair) * half_width + core * features, 1
    )
    sums = lax.psum(
        jnp.concatenate([spread, grad_gain_mix[None], grad_gain_ffn[None]], axis=0),
        ("seq", "wshard"),
    )
    sums = lax.dynamic_slice_in_dim(sums, pair * half_width, half_width, 1)
    return (
        block_out.reshape(groups, block, width),
        grad_hidden,
        out_in,
        out_out,
        out_gate,
        out_up,
        out_down,
        sums[:3],
        sums[3],
        sums[4],
    )


def solution(mesh):
    return jax.shard_map(
        local,
        mesh=mesh,
        in_specs=(
            P("wshard", "seq", None),
            P("wshard", "seq"),
            P("wshard", "seq", None),
            P(None, None, "wshard"),
            P("wshard", None),
            P(None, "wshard"),
            P(None, "wshard"),
            P("wshard", None),
            P(None, "wshard"),
            P("wshard"),
            P("wshard"),
        ),
        out_specs=(
            P("wshard", "seq", None),
            P("wshard", "seq", None),
            P("seq", None, "wshard"),
            P("wshard", "seq"),
            P("seq", "wshard"),
            P("seq", "wshard"),
            P("wshard", "seq"),
            P(None, "wshard"),
            P("wshard"),
            P("wshard"),
        ),
        check_vma=False,
    )
```

profile of v0, /device:TPU:0, one launch (start us, length us, event | category | flops | bytes accessed | tf_op | source)
XLA Modules:
  0.0 517.6 jit_solution(11000948463357092600)
XLA Ops:
  12.7 4.7 collective-permute-start.7
  21.6 25.2 %collective-permute-done.1 = bf16[5,512]{1,0:T(8,128)(2,1)S(1)} collective-permute-done((bf16[5,512]{1,0:T(8,128)(2,1)S(1)}, bf16[5,512]{1,0:T(8,128)(2,1)S(1)}, u32[]{:S(2)}, u32[]{:S(2)}) %collective-permute-start.1) | collective-permute-done | bytes 5152 | tf_op jit(solution)/shard_map/ppermute | solution.py:24
  63.7 5.4 %fusion.73 = f32[1024,1536]{1,0:T(8,128)S(1)} fusion(bf16[1024,1536]{1,0:T(8,128)(2,1)} %fusion.75, f32[1024]{0:T(1024)S(1)} %bitcast.190, f32[1024]{0:T(1024)S(1)} %add_rsqrt_fusion.1, bf16[512,1024]{1,0:T(8,128)(2,1)S(1)} %collective-permute-done, bf16[512,1024]{1,0:T(8,128)(2,1)S(1)} %bitcast.148), kind=kOutput, calls=%fused_computation.131 | convolution fusion | flops 3228565504 | bytes 11542528 | tf_op jit(solution)/shard_map/dot_general | solution.py:32
  73.1 4.2 convolution_convert_fusion.4
  79.7 23.4 %collective-permute-done.17 = bf16[512,1024]{1,0:T(8,128)(2,1)} collective-permute-done((bf16[512,1024]{1,0:T(8,128)(2,1)}, bf16[512,1024]{1,0:T(8,128)(2,1)}, u32[]{:S(2)}, u32[]{:S(2)}) %collective-permute-start.17) | collective-permute-done | bytes 1048608 | tf_op jit(solution)/shard_map/ppermute | solution.py:24
  113.5 4.5 fusion.61
  118.0 4.5 fusion.69
  122.6 9.7 %multiply_convert_fusion.2 = (bf16[1024,1152]{1,0:T(8,128)(2,1)S(1)}, bf16[1024,1152]{1,0:T(8,128)(2,1)}, bf16[1024,1152]{1,0:T(8,128)(2,1)}) fusion(f32[1024,1152]{1,0:T(8,128)} %fusion.69, f32[1024,1152]{1,0:T(8,128)} %fusion.61, bf16[2304,1024]{1,0:T(8,128)(2,1)S(1)} %bitcast.220, s32[]{:T(128)S(6)} %select_n.227, ...), kind=kOutput, calls=%fused_computation.14 | convolution fusion | flops 2437808128 | bytes 20971524 | tf_op jit(solution)/shard_map/dot_general | solution.py:40
  132.3 6.1 %fusion.65 = f32[1024,1024]{1,0:T(8,128)S(1)} fusion(bf16[1024,1152]{1,0:T(8,128)(2,1)} %get-tuple-element.24, bf16[1024,2304]{1,0:T(8,128)(2,1)} %param.16, s32[]{:T(128)S(6)} %select_n.227), kind=kOutput, calls=%fused_computation.113 | convolution fusion | flops 2415919104 | bytes 8912900 | tf_op jit(solution)/shard_map/dot_general | solution.py:40
  138.8 5.0 add_convert_fusion.1
  149.6 4.5 fusion.59
  154.1 4.5 fusion.67
  158.6 11.4 %multiply_convert_fusion = (bf16[1024,1152]{1,0:T(8,128)(2,1)S(1)}, bf16[1024,1152]{1,0:T(8,128)(2,1)}, bf16[1024,1152]{1,0:T(8,128)(2,1)}) fusion(f32[1024,1152]{1,0:T(8,128)} %fusion.67, f32[1024,1152]{1,0:T(8,128)} %fusion.59, bf16[2304,1024]{1,0:T(8,128)(2,1)} %param.18, s32[]{:T(128)S(6)} %select_n.227, bf16[512,1024]{1,0:T(8,128)(2,1)} %collective-permute-done.18, ...), kind=kOutput, calls=%fused_computation.12 | convolution fusion | flops 2437808128 | bytes 20971524 | tf_op jit(solution)/shard_map/dot_general | solution.py:40
  170.1 6.1 %convolution_convert_fusion.1 = bf16[1024,1024]{1,0:T(8,128)(2,1)S(1)} fusion(bf16[1024,1152]{1,0:T(8,128)(2,1)} %get-tuple-element.28, bf16[2304,1024]{1,0:T(8,128)(2,1)} %param.18, s32[]{:T(128)S(6)} %select_n.227), kind=kOutput, calls=%fused_computation.96 | convolution fusion | flops 2416967680 | bytes 6815748 | tf_op jit(solution)/shard_map/dot_general | solution.py:32
  177.6 4.6 fusion.63
  187.7 9.3 %fusion.21 = bf16[1024,1152]{1,0:T(8,128)(2,1)S(1)} fusion(bf16[1024,1152]{1,0:T(8,128)(2,1)} %get-tuple-element.28, bf16[1024,1152]{1,0:T(8,128)(2,1)} %get-tuple-element.25, bf16[512,1024]{1,0:T(8,128)(2,1)} %collective-permute-done.18, bf16[512,1024]{1,0:T(8,128)(2,1)} %collective-permute-done.17, bf16[512,1024]{1,0:T(8,128)(2,1)} %collective-permute-done.15, ...), kind=kOutput, calls=%fused_computation.37 | convolution fusion | flops 4859232256 | bytes 11272192 | tf_op jit(solution)/shard_map/dot_general | solution.py:36
  199.9 8.2 %fusion.26 = bf16[1024,1152]{1,0:T(8,128)(2,1)S(1)} fusion(bf16[1024,1152]{1,0:T(8,128)(2,1)} %copy-done.38, bf16[1024,1152]{1,0:T(8,128)(2,1)} %copy-done.37, bf16[512,1024]{1,0:T(8,128)(2,1)S(1)} %collective-permute-done.12, bf16[512,1024]{1,0:T(8,128)(2,1)S(1)} %collective-permute-done.11, bf16[1024,1024]{1,0:T(8,128)(2,1)S(1)} %multiply_convert_fusion.6), kind=kOutput, calls=%fused_computation.38 | convolution fusion | flops 4855037952 | bytes 11272192 | tf_op jit(solution)/shard_map/dot_general | solution.py:36
  210.2 8.8 %fusion.29 = bf16[1024,1152]{1,0:T(8,128)(2,1)S(1)} fusion(bf16[1024,1152]{1,0:T(8,128)(2,1)} %get-tuple-element.27, bf16[1024,1152]{1,0:T(8,128)(2,1)} %get-tuple-element.24, bf16[512,1024]{1,0:T(8,128)(2,1)} %copy-done.24, bf16[512,1024]{1,0:T(8,128)(2,1)} %copy-done.23, bf16[1024,1024]{1,0:T(8,128)(2,1)S(1)} %multiply_convert_fusion.6), kind=kOutput, calls=%fused_computation.39 | convolution fusion | flops 4855037952 | bytes 11272192 | tf_op jit(solution)/shard_map/dot_general | solution.py:36
  229.3 23.5 %collective-permute-done.34 = bf16[4,128,1152]{2,1,0:T(8,128)(2,1)} collective-permute-done((bf16[4,128,1152]{2,1,0:T(8,128)(2,1)}, bf16[4,128,1152]{2,1,0:T(8,128)(2,1)}, u32[]{:S(2)}, u32[]{:S(2)}) %collective-permute-start.34) | collective-permute-done | bytes 1179680 | tf_op jit(solution)/shard_map/ppermute | solution.py:12
  255.6 21.7 %collective-permute-done.30 = bf16[4,128,1152]{2,1,0:T(8,128)(2,1)S(1)} collective-permute-done((bf16[4,128,1152]{2,1,0:T(8,128)(2,1)S(1)}, bf16[4,128,1152]{2,1,0:T(8,128)(2,1)S(1)}, u32[]{:S(2)}, u32[]{:S(2)}) %collective-permute-start.30) | collective-permute-done | bytes 1179680 | tf_op jit(solution)/shard_map/ppermute | solution.py:12
  280.6 12.9 %collective-permute-done.35 = bf16[2,128,1152]{2,1,0:T(8,128)(2,1)S(1)} collective-permute-done((bf16[2,128,1152]{2,1,0:T(8,128)(2,1)S(1)}, bf16[2,128,1152]{2,1,0:T(8,128)(2,1)S(1)}, u32[]{:S(2)}, u32[]{:S(2)}) %collective-permute-start.35) | collective-permute-done | bytes 589856 | tf_op jit(solution)/shard_map/ppermute | solution.py:12
  295.3 9.3 %collective-permute-done.31 = bf16[2,128,1152]{2,1,0:T(8,128)(2,1)S(1)} collective-permute-done((bf16[2,128,1152]{2,1,0:T(8,128)(2,1)S(1)}, bf16[2,128,1152]{2,1,0:T(8,128)(2,1)S(1)}, u32[]{:S(2)}, u32[]{:S(2)}) %collective-permute-start.31) | collective-permute-done | bytes 589856 | tf_op jit(solution)/shard_map/ppermute | solution.py:12
  307.3 11.9 %collective-permute-done.40 = bf16[1,128,1152]{2,1,0:T(8,128)(2,1)S(1)} collective-permute-done((bf16[1,128,1152]{2,1,0:T(8,128)(2,1)S(1)}, bf16[1,128,1152]{2,1,0:T(8,128)(2,1)S(1)}, u32[]{:S(2)}, u32[]{:S(2)}) %collective-permute-start.40) | collective-permute-done | bytes 294944 | tf_op jit(solution)/shard_map/ppermute | solution.py:12
  320.3 14.0 %collective-permute-done.36 = bf16[1,128,1152]{2,1,0:T(8,128)(2,1)S(1)} collective-permute-done((bf16[1,128,1152]{2,1,0:T(8,128)(2,1)S(1)}, bf16[1,128,1152]{2,1,0:T(8,128)(2,1)S(1)}, u32[]{:S(2)}, u32[]{:S(2)}) %collective-permute-start.36) | collective-permute-done | bytes 294944 | tf_op jit(solution)/shard_map/ppermute | solution.py:12
  336.9 11.6 %collective-permute-done.32 = bf16[1,128,1152]{2,1,0:T(8,128)(2,1)S(1)} collective-permute-done((bf16[1,128,1152]{2,1,0:T(8,128)(2,1)S(1)}, bf16[1,128,1152]{2,1,0:T(8,128)(2,1)S(1)}, u32[]{:S(2)}, u32[]{:S(2)}) %collective-permute-start.32) | collective-permute-done | bytes 294944 | tf_op jit(solution)/shard_map/ppermute | solution.py:12
  349.6 4.0 fusion.122
  366.2 4.6 multiply_reduce_fusion.6
  377.0 3.7 convolution_convert_fusion
  389.9 40.0 %collective-permute-done.25 = bf16[8,128,1024]{2,1,0:T(8,128)(2,1)S(1)} collective-permute-done((bf16[8,128,1024]{2,1,0:T(8,128)(2,1)S(1)}, bf16[8,128,1024]{2,1,0:T(8,128)(2,1)S(1)}, u32[]{:S(2)}, u32[]{:S(2)}) %collective-permute-start.25) | collective-permute-done | bytes 2097184 | tf_op jit(solution)/shard_map/ppermute | solution.py:24
  435.1 21.7 %collective-permute-done.26 = bf16[4,128,1024]{2,1,0:T(8,128)(2,1)S(1)} collective-permute-done((bf16[4,128,1024]{2,1,0:T(8,128)(2,1)S(1)}, bf16[4,128,1024]{2,1,0:T(8,128)(2,1)S(1)}, u32[]{:S(2)}, u32[]{:S(2)}) %collective-permute-start.26) | collective-permute-done | bytes 1048608 | tf_op jit(solution)/shard_map/ppermute | solution.py:12
  459.2 11.3 %collective-permute-done.27 = bf16[2,128,1024]{2,1,0:T(8,128)(2,1)S(1)} collective-permute-done((bf16[2,128,1024]{2,1,0:T(8,128)(2,1)S(1)}, bf16[2,128,1024]{2,1,0:T(8,128)(2,1)S(1)}, u32[]{:S(2)}, u32[]{:S(2)}) %collective-permute-start.27) | collective-permute-done | bytes 524320 | tf_op jit(solution)/shard_map/ppermute | solution.py:12
  471.4 40.1 %psum.7 = f32[5,1024]{1,0:T(8,128)S(1)} all-reduce(f32[5,1024]{1,0:T(8,128)S(1)} %pad_maximum_fusion.23), channel_id=1, replica_groups=mesh['seq'=16,'wshard'=2] {'seq','wshard'}, use_global_device_ids=true, to_apply=%region_10.11 | all-reduce | flops 5120 | bytes 40960 | tf_op jit(solution)/shard_map/psum | solution.py:347
  (342 shorter events, 135.0 us)
Async XLA Ops:
  5.7 41.8 %collective-permute-start.5 = (bf16[4,2,1152]{2,0,1:T(4,128)(2,1)S(1)}, bf16[4,2,1152]{2,0,1:T(4,128)(2,1)S(1)}, u32[]{:S(2)}, u32[]{:S(2)}) collective-permute-start(bf16[4,2,1152]{2,0,1:T(4,128)(2,1)S(1)} %get-tuple-element.69), channel_id=1, source_target_pairs={{4,0},{8,4},{12,8},{16,12},{20,16},{24,20},{28,24},{5,1},{9,5},{13... | collective-permute-start | bytes 55304 | tf_op jit(solution)/shard_map/ppermute | solution.py:12
  7.0 41.0 %collective-permute-start.6 = (bf16[4,2,1152]{2,0,1:T(4,128)(2,1)S(1)}, bf16[4,2,1152]{2,0,1:T(4,128)(2,1)S(1)}, u32[]{:S(2)}, u32[]{:S(2)}) collective-permute-start(bf16[4,2,1152]{2,0,1:T(4,128)(2,1)S(1)} %get-tuple-element.69), channel_id=1, source_target_pairs={{4,2},{8,6},{12,10},{16,14},{20,18},{24,22},{28,26},{5,3},{9,7},{1... | collective-permute-start | bytes 55304 | tf_op jit(solution)/shard_map/ppermute | solution.py:12
  9.0 42.0 %collective-permute-start.2 = (bf16[3,1024,256]{2,1,0:T(8,128)(2,1)}, bf16[3,1024,256]{2,1,0:T(8,128)(2,1)}, u32[]{:S(2)}, u32[]{:S(2)}) collective-permute-start(bf16[3,1024,256]{2,1,0:T(8,128)(2,1)} %dynamic-slice_bitcast_fusion), channel_id=1, source_target_pairs={{0,1},{1,0},{2,3},{3,2},{4,5},{5,4},{6,7},{7,6},{8,9},{9,8},{10,11... | collective-permute-start | bytes 4718600 | tf_op jit(solution)/shard_map/ppermute | solution.py:24
  11.9 37.5 %collective-permute-start.3 = (bf16[4,2,1152]{2,0,1:T(4,128)(2,1)S(1)}, bf16[4,2,1152]{2,0,1:T(4,128)(2,1)S(1)}, u32[]{:S(2)}, u32[]{:S(2)}) collective-permute-start(bf16[4,2,1152]{2,0,1:T(4,128)(2,1)S(1)} %get-tuple-element.68), channel_id=1, source_target_pairs={{2,4},{6,8},{10,12},{14,16},{18,20},{22,24},{26,28},{3,5},{7,9},{1... | collective-permute-start | bytes 55304 | tf_op jit(solution)/shard_map/ppermute | solution.py:12
  21.3 25.4 %collective-permute-start.1 = (bf16[5,512]{1,0:T(8,128)(2,1)S(1)}, bf16[5,512]{1,0:T(8,128)(2,1)S(1)}, u32[]{:S(2)}, u32[]{:S(2)}) collective-permute-start(bf16[5,512]{1,0:T(8,128)(2,1)S(1)} %pad_maximum_fusion.26), channel_id=1, source_target_pairs={{0,1},{1,0},{2,3},{3,2},{4,5},{5,4},{6,7},{7,6},{8,9},{9,8},{10,11... | collective-permute-start | bytes 15368 | tf_op jit(solution)/shard_map/ppermute | solution.py:24
  48.0 25.1 %collective-permute-start.8 = (bf16[256,1024]{1,0:T(8,128)(2,1)}, bf16[256,1024]{1,0:T(8,128)(2,1)}, u32[]{:S(2)}, u32[]{:S(2)}) collective-permute-start(bf16[256,1024]{1,0:T(8,128)(2,1)} %constant_dynamic-slice_fusion.25), channel_id=1, source_target_pairs={{0,1},{1,0},{2,3},{3,2},{4,5},{5,4},{6,7},{7,6},{8,9},{9,8},{10,11... | collective-permute-start | bytes 1572872 | tf_op jit(solution)/shard_map/ppermute | solution.py:24
  77.2 29.5 %collective-permute-start.9 = (bf16[1024,1024]{1,0:T(8,128)(2,1)}, bf16[1024,1024]{1,0:T(8,128)(2,1)}, u32[]{:S(2)}, u32[]{:S(2)}) collective-permute-start(bf16[1024,1024]{1,0:T(8,128)(2,1)} %convolution_convert_fusion.4), channel_id=1, source_target_pairs={{0,2},{2,0},{4,6},{6,4},{8,10},{10,8},{12,14},{14,12},{16,18},{18,... | collective-permute-start | bytes 6291464 | tf_op jit(solution)/shard_map/ppermute | solution.py:12
  77.5 25.7 %collective-permute-start.17 = (bf16[512,1024]{1,0:T(8,128)(2,1)}, bf16[512,1024]{1,0:T(8,128)(2,1)}, u32[]{:S(2)}, u32[]{:S(2)}) collective-permute-start(bf16[512,1024]{1,0:T(8,128)(2,1)} %bitcast.18), channel_id=1, source_target_pairs={{0,1},{1,0},{2,3},{3,2},{4,5},{5,4},{6,7},{7,6},{8,9},{9,8},{10,11... | collective-permute-start | bytes 3145736 | tf_op jit(solution)/shard_map/ppermute | solution.py:24
  78.9 43.6 %collective-permute-start.15 = (bf16[512,1024]{1,0:T(8,128)(2,1)}, bf16[512,1024]{1,0:T(8,128)(2,1)}, u32[]{:S(2)}, u32[]{:S(2)}) collective-permute-start(bf16[512,1024]{1,0:T(8,128)(2,1)} %bitcast.18), channel_id=1, source_target_pairs={{0,2},{2,0},{4,6},{6,4},{8,10},{10,8},{12,14},{14,12},{16,18},{18,... | collective-permute-start | bytes 3145736 | tf_op jit(solution)/shard_map/ppermute | solution.py:12
  103.1 55.5 %collective-permute-start.18 = (bf16[512,1024]{1,0:T(8,128)(2,1)}, bf16[512,1024]{1,0:T(8,128)(2,1)}, u32[]{:S(2)}, u32[]{:S(2)}) collective-permute-start(bf16[512,1024]{1,0:T(8,128)(2,1)} %collective-permute-done.17), channel_id=1, source_target_pairs={{0,2},{2,0},{4,6},{6,4},{8,10},{10,8},{12,14},{14,12},{16,18},{18,... | collective-permute-start | bytes 3145736 | tf_op jit(solution)/shard_map/ppermute | solution.py:12
  111.9 26.5 %collective-permute-start.11 = (bf16[512,1024]{1,0:T(8,128)(2,1)S(1)}, bf16[512,1024]{1,0:T(8,128)(2,1)S(1)}, u32[]{:S(2)}, u32[]{:S(2)}) collective-permute-start(bf16[512,1024]{1,0:T(8,128)(2,1)S(1)} %slice.503), channel_id=1, source_target_pairs={{0,1},{1,0},{2,3},{3,2},{4,5},{5,4},{6,7},{7,6},{8,9},{9,8},{10,11... | collective-permute-start | bytes 3145736 | tf_op jit(solution)/shard_map/ppermute | solution.py:24
  144.8 203.8 %collective-permute-start.16 = (bf16[512,1024]{1,0:T(8,128)(2,1)}, bf16[512,1024]{1,0:T(8,128)(2,1)S(1)}, u32[]{:S(2)}, u32[]{:S(2)}) collective-permute-start(bf16[512,1024]{1,0:T(8,128)(2,1)} %slice.507), channel_id=1, source_target_pairs={{0,2},{2,0},{4,6},{6,4},{8,10},{10,8},{12,14},{14,12},{16,18},{18,... | collective-permute-start | bytes 3145736 | tf_op jit(solution)/shard_map/ppermute | solution.py:12
  177.3 42.1 %collective-permute-start.13 = (bf16[512,1024]{1,0:T(8,128)(2,1)}, bf16[512,1024]{1,0:T(8,128)(2,1)}, u32[]{:S(2)}, u32[]{:S(2)}) collective-permute-start(bf16[512,1024]{1,0:T(8,128)(2,1)} %slice.505), channel_id=1, source_target_pairs={{0,2},{2,0},{4,6},{6,4},{8,10},{10,8},{12,14},{14,12},{16,18},{18,... | collective-permute-start | bytes 3145736 | tf_op jit(solution)/shard_map/ppermute | solution.py:12
  187.4 35.1 %collective-permute-start.19 = (bf16[512,1024]{1,0:T(8,128)(2,1)}, bf16[512,1024]{1,0:T(8,128)(2,1)}, u32[]{:S(2)}, u32[]{:S(2)}) collective-permute-start(bf16[512,1024]{1,0:T(8,128)(2,1)} %slice.509), channel_id=1, source_target_pairs={{0,2},{2,0},{4,6},{6,4},{8,10},{10,8},{12,14},{14,12},{16,18},{18,... | collective-permute-start | bytes 3145736 | tf_op jit(solution)/shard_map/ppermute | solution.py:12
  198.4 29.1 %collective-permute-start.38 = (bf16[4,128,1152]{2,1,0:T(8,128)(2,1)}, bf16[4,128,1152]{2,1,0:T(8,128)(2,1)}, u32[]{:S(2)}, u32[]{:S(2)}) collective-permute-start(bf16[4,128,1152]{2,1,0:T(8,128)(2,1)} %pad_maximum_fusion.16), channel_id=1, source_target_pairs={{0,4},{2,6},{4,0},{6,2},{8,12},{10,14},{12,8},{14,10},{16,20},{18,... | collective-permute-start | bytes 3538952 | tf_op jit(solution)/shard_map/ppermute | solution.py:12
  209.7 43.1 %collective-permute-start.34 = (bf16[4,128,1152]{2,1,0:T(8,128)(2,1)}, bf16[4,128,1152]{2,1,0:T(8,128)(2,1)}, u32[]{:S(2)}, u32[]{:S(2)}) collective-permute-start(bf16[4,128,1152]{2,1,0:T(8,128)(2,1)} %pad_maximum_fusion.15), channel_id=1, source_target_pairs={{0,4},{2,6},{4,0},{6,2},{8,12},{10,14},{12,8},{14,10},{16,20},{18,... | collective-permute-start | bytes 3538952 | tf_op jit(solution)/shard_map/ppermute | solution.py:12
  220.2 129.4 %collective-permute-start.10 = (bf16[512,1024]{1,0:T(8,128)(2,1)S(1)}, bf16[512,1024]{1,0:T(8,128)(2,1)S(1)}, u32[]{:S(2)}, u32[]{:S(2)}) collective-permute-start(bf16[512,1024]{1,0:T(8,128)(2,1)S(1)} %copy-done.22), channel_id=1, source_target_pairs={{0,2},{2,0},{4,6},{6,4},{8,10},{10,8},{12,14},{14,12},{16,18},{18,... | collective-permute-start | bytes 3145736 | tf_op jit(solution)/shard_map/ppermute | solution.py:12
  222.5 54.8 %collective-permute-start.30 = (bf16[4,128,1152]{2,1,0:T(8,128)(2,1)S(1)}, bf16[4,128,1152]{2,1,0:T(8,128)(2,1)S(1)}, u32[]{:S(2)}, u32[]{:S(2)}) collective-permute-start(bf16[4,128,1152]{2,1,0:T(8,128)(2,1)S(1)} %pad_maximum_fusion.14), channel_id=1, source_target_pairs={{0,4},{2,6},{4,0},{6,2},{8,12},{10,14},{12,8},{14,10},{16,20},{18,... | collective-permute-start | bytes 3538952 | tf_op jit(solution)/shard_map/ppermute | solution.py:12
  227.5 122.1 %collective-permute-start.14 = (bf16[512,1024]{1,0:T(8,128)(2,1)S(1)}, bf16[512,1024]{1,0:T(8,128)(2,1)S(1)}, u32[]{:S(2)}, u32[]{:S(2)}) collective-permute-start(bf16[512,1024]{1,0:T(8,128)(2,1)S(1)} %add_convert_fusion.5), channel_id=1, source_target_pairs={{0,1},{1,0},{2,3},{3,2},{4,5},{5,4},{6,7},{7,6},{8,9},{9,8},{10,11... | collective-permute-start | bytes 3145736 | tf_op jit(solution)/shard_map/ppermute | solution.py:24
  252.8 26.2 %collective-permute-start.39 = (bf16[2,128,1152]{2,1,0:T(8,128)(2,1)S(1)}, bf16[2,128,1152]{2,1,0:T(8,128)(2,1)S(1)}, u32[]{:S(2)}, u32[]{:S(2)}) collective-permute-start(bf16[2,128,1152]{2,1,0:T(8,128)(2,1)S(1)} %add_convert_fusion.6), channel_id=1, source_target_pairs={{0,8},{2,10},{4,12},{6,14},{8,0},{10,2},{12,4},{14,6},{16,24},{18,... | collective-permute-start | bytes 1769480 | tf_op jit(solution)/shard_map/ppermute | solution.py:12
  277.3 16.3 %collective-permute-start.35 = (bf16[2,128,1152]{2,1,0:T(8,128)(2,1)S(1)}, bf16[2,128,1152]{2,1,0:T(8,128)(2,1)S(1)}, u32[]{:S(2)}, u32[]{:S(2)}) collective-permute-start(bf16[2,128,1152]{2,1,0:T(8,128)(2,1)S(1)} %add_convert_fusion.7), channel_id=1, source_target_pairs={{0,8},{2,10},{4,12},{6,14},{8,0},{10,2},{12,4},{14,6},{16,24},{18,... | collective-permute-start | bytes 1769480 | tf_op jit(solution)/shard_map/ppermute | solution.py:12
  279.0 25.6 %collective-permute-start.31 = (bf16[2,128,1152]{2,1,0:T(8,128)(2,1)S(1)}, bf16[2,128,1152]{2,1,0:T(8,128)(2,1)S(1)}, u32[]{:S(2)}, u32[]{:S(2)}) collective-permute-start(bf16[2,128,1152]{2,1,0:T(8,128)(2,1)S(1)} %add_convert_fusion.8), channel_id=1, source_target_pairs={{0,8},{2,10},{4,12},{6,14},{8,0},{10,2},{12,4},{14,6},{16,24},{18,... | collective-permute-start | bytes 1769480 | tf_op jit(solution)/shard_map/ppermute | solution.py:12
  293.6 55.1 %collective-permute-start.20 = (bf16[512,1024]{1,0:T(8,128)(2,1)S(1)}, bf16[512,1024]{1,0:T(8,128)(2,1)S(1)}, u32[]{:S(2)}, u32[]{:S(2)}) collective-permute-start(bf16[512,1024]{1,0:T(8,128)(2,1)S(1)} %add_convert_fusion.3), channel_id=1, source_target_pairs={{0,1},{1,0},{2,3},{3,2},{4,5},{5,4},{6,7},{7,6},{8,9},{9,8},{10,11... | collective-permute-start | bytes 3145736 | tf_op jit(solution)/shard_map/ppermute | solution.py:24
  304.6 14.6 %collective-permute-start.40 = (bf16[1,128,1152]{2,1,0:T(8,128)(2,1)S(1)}, bf16[1,128,1152]{2,1,0:T(8,128)(2,1)S(1)}, u32[]{:S(2)}, u32[]{:S(2)}) collective-permute-start(bf16[1,128,1152]{2,1,0:T(8,128)(2,1)S(1)} %add_convert_fusion.10), channel_id=1, source_target_pairs={{0,16},{2,18},{4,20},{6,22},{8,24},{10,26},{12,28},{14,30},{16,0},... | collective-permute-start | bytes 884744 | tf_op jit(solution)/shard_map/ppermute | solution.py:12
  319.2 15.1 %collective-permute-start.36 = (bf16[1,128,1152]{2,1,0:T(8,128)(2,1)S(1)}, bf16[1,128,1152]{2,1,0:T(8,128)(2,1)S(1)}, u32[]{:S(2)}, u32[]{:S(2)}) collective-permute-start(bf16[1,128,1152]{2,1,0:T(8,128)(2,1)S(1)} %add_convert_fusion.11), channel_id=1, source_target_pairs={{0,16},{2,18},{4,20},{6,22},{8,24},{10,26},{12,28},{14,30},{16,0},... | collective-permute-start | bytes 884744 | tf_op jit(solution)/shard_map/ppermute | solution.py:12
  334.3 14.2 %collective-permute-start.32 = (bf16[1,128,1152]{2,1,0:T(8,128)(2,1)S(1)}, bf16[1,128,1152]{2,1,0:T(8,128)(2,1)S(1)}, u32[]{:S(2)}, u32[]{:S(2)}) collective-permute-start(bf16[1,128,1152]{2,1,0:T(8,128)(2,1)S(1)} %add_convert_fusion.12), channel_id=1, source_target_pairs={{0,16},{2,18},{4,20},{6,22},{8,24},{10,26},{12,28},{14,30},{16,0},... | collective-permute-start | bytes 884744 | tf_op jit(solution)/shard_map/ppermute | solution.py:12
  353.6 12.6 %collective-permute-start.21 = (bf16[512,1024]{1,0:T(8,128)(2,1)}, bf16[512,1024]{1,0:T(8,128)(2,1)}, u32[]{:S(2)}, u32[]{:S(2)}) collective-permute-start(bf16[512,1024]{1,0:T(8,128)(2,1)} %get-tuple-element.19), channel_id=1, source_target_pairs={{0,2},{2,0},{4,6},{6,4},{8,10},{10,8},{12,14},{14,12},{16,18},{18,... | collective-permute-start | bytes 3145736 | tf_op jit(solution)/shard_map/ppermute | solution.py:12
  381.5 48.4 %collective-permute-start.25 = (bf16[8,128,1024]{2,1,0:T(8,128)(2,1)S(1)}, bf16[8,128,1024]{2,1,0:T(8,128)(2,1)S(1)}, u32[]{:S(2)}, u32[]{:S(2)}) collective-permute-start(bf16[8,128,1024]{2,1,0:T(8,128)(2,1)S(1)} %dynamic-slice_dynamic-update-slice_fusion), channel_id=1, source_target_pairs={{0,1},{1,0},{2,3},{3,2},{4,5},{5,4},{6,7},{7,6},{8,9},{9,8},{10,11... | collective-permute-start | bytes 6291464 | tf_op jit(solution)/shard_map/ppermute | solution.py:24
  388.5 45.7 %collective-permute-start.24 = (bf16[512,1024]{1,0:T(8,128)(2,1)S(1)}, bf16[512,1024]{1,0:T(8,128)(2,1)S(1)}, u32[]{:S(2)}, u32[]{:S(2)}) collective-permute-start(bf16[512,1024]{1,0:T(8,128)(2,1)S(1)} %slice.522), channel_id=1, source_target_pairs={{0,2},{2,0},{4,6},{6,4},{8,10},{10,8},{12,14},{14,12},{16,18},{18,... | collective-permute-start | bytes 3145736 | tf_op jit(solution)/shard_map/ppermute | solution.py:12
  430.3 26.4 %collective-permute-start.26 = (bf16[4,128,1024]{2,1,0:T(8,128)(2,1)S(1)}, bf16[4,128,1024]{2,1,0:T(8,128)(2,1)S(1)}, u32[]{:S(2)}, u32[]{:S(2)}) collective-permute-start(bf16[4,128,1024]{2,1,0:T(8,128)(2,1)S(1)} %add_convert_fusion.2), channel_id=1, source_target_pairs={{0,4},{2,6},{4,0},{6,2},{8,12},{10,14},{12,8},{14,10},{16,20},{18,... | collective-permute-start | bytes 3145736 | tf_op jit(solution)/shard_map/ppermute | solution.py:12
  457.0 13.5 %collective-permute-start.27 = (bf16[2,128,1024]{2,1,0:T(8,128)(2,1)S(1)}, bf16[2,128,1024]{2,1,0:T(8,128)(2,1)S(1)}, u32[]{:S(2)}, u32[]{:S(2)}) collective-permute-start(bf16[2,128,1024]{2,1,0:T(8,128)(2,1)S(1)} %add_convert_fusion.9), channel_id=1, source_target_pairs={{0,8},{2,10},{4,12},{6,14},{8,0},{10,2},{12,4},{14,6},{16,24},{18,... | collective-permute-start | bytes 1572872 | tf_op jit(solution)/shard_map/ppermute | solution.py:12
  471.3 41.4 %collective-permute-start.28 = (bf16[1,128,1024]{2,1,0:T(8,128)(2,1)S(1)}, bf16[1,128,1024]{2,1,0:T(8,128)(2,1)S(1)}, u32[]{:S(2)}, u32[]{:S(2)}) collective-permute-start(bf16[1,128,1024]{2,1,0:T(8,128)(2,1)S(1)} %add_convert_fusion.13), channel_id=1, source_target_pairs={{0,16},{2,18},{4,20},{6,22},{8,24},{10,26},{12,28},{14,30},{16,0},... | collective-permute-start | bytes 786440 | tf_op jit(solution)/shard_map/ppermute | solution.py:12
  (65 other events, 660.7 us)
where the time goes:
time: 524 us; the launch traced here: 518 us
  waiting for transfers between devices  232 us (44%)
  matrix products  122 us (23%)
  other arithmetic  46 us (9%)
  blocking collectives  40.1 us (8%)
  local copies, waits for them, and re-layouts  38.7 us (7%)
  starting transfers between devices  36 us (7%)
    ppermute x34, waiting for transfers between devices, over_seq(): return lax.ppermute(block, 'seq', route)  144 us
    ppermute x8, waiting for transfers between devices, swap_pair(): return lax.ppermute(block, 'wshard', [(0, 1), (1, 0)])  88.6 us
    dot_general x9, matrix products, mm_nt(): lax.dot_general(left, right, (((1,), (1,)), ((), ())), preferred_element_...  50.2 us
    psum x1, blocking collectives, local(): lax.psum(jnp.concatenate([spread, grad_gain_mix[None], grad_gain_ffn[None...  40.1 us
    dot_general x9, matrix products, mm(): return jnp.dot(left, right, preferred_element_type=F32)  39.3 us
    dot_general x5, matrix products, mm_tn(): lax.dot_general(left, right, (((0,), (0,)), ((), ())), preferred_element_...  32.9 us
    ppermute x34, starting transfers between devices, over_seq(): return lax.ppermute(block, 'seq', route)  26.3 us
    unnamed x125, local copies, waits for them, and re-layouts  18.5 us
  transfers between devices with their start and end apart: 42, of which 15 were waited for; matrix products, arithmetic and copies ran while one was open for 33% of the time, Pallas kernels for 0%

commit v1 on v0

--- a/solution.py
+++ b/solution.py
@@ -344,10 +344,10 @@
     spread = lax.dynamic_update_slice_in_dim(
         spread, grad_taps[:, features:], (1 - pair) * half_width + core * features, 1
     )
-    sums = lax.psum(
-        jnp.concatenate([spread, grad_gain_mix[None], grad_gain_ffn[None]], axis=0),
-        ("seq", "wshard"),
-    )
+    one_axis = lax.psum(
+        jnp.concatenate([spread, grad_gain_mix[None], grad_gain_ffn[None]], axis=0), "wshard"
+    )
+    sums = lax.psum(one_axis, "seq")
     sums = lax.dynamic_slice_in_dim(sums, pair * half_width, half_width, 1)
     return (
         block_out.reshape(groups, block, width),

time: 524 us -> 549 us (1.048)
  blocking collectives: 40.1 us -> 65.3 us
    psum x0 -> x1, blocking collectives: none -> 57.6 us  [local(): sums = lax.psum(one_axis, 'seq')]
    psum x1, blocking collectives: 40.1 us -> 7.63 us  [local(): lax.psum(jnp.concatenate([spread, grad_gain_mix[None], grad_gain_ffn[None...]
  transfers between devices with their start and end apart: 42 -> 42, of which waited for: 15 -> 15; matrix products, arithmetic and copies ran while one was open for 33% -> 31% of each run, Pallas kernels for 0% -> 0%
where the time goes in v1:
time: 549 us; the launch traced here: 543 us
  waiting for transfers between devices  232 us (42%)
  matrix products  122 us (22%)
  blocking collectives  65.3 us (12%)
  other arithmetic  46 us (8%)
  local copies, waits for them, and re-layouts  38.6 us (7%)
  starting transfers between devices  35.8 us (7%)
    ppermute x34, waiting for transfers between devices, over_seq(): return lax.ppermute(block, 'seq', route)  144 us
    ppermute x8, waiting for transfers between devices, swap_pair(): return lax.ppermute(block, 'wshard', [(0, 1), (1, 0)])  88.7 us
    psum x1, blocking collectives, local(): sums = lax.psum(one_axis, 'seq')  57.6 us
    dot_general x9, matrix products, mm_nt(): lax.dot_general(left, right, (((1,), (1,)), ((), ())), preferred_element_...  50.3 us
    dot_general x9, matrix products, mm(): return jnp.dot(left, right, preferred_element_type=F32)  39.3 us
    dot_general x5, matrix products, mm_tn(): lax.dot_general(left, right, (((0,), (0,)), ((), ())), preferred_element_...  32.9 us
    ppermute x34, starting transfers between devices, over_seq(): return lax.ppermute(block, 'seq', route)  26.3 us
    unnamed x125, local copies, waits for them, and re-layouts  18.5 us
  transfers between devices with their start and end apart: 42, of which 15 were waited for; matrix products, arithmetic and copies ran while one was open for 31% of the time, Pallas kernels for 0%

profile of v1, /device:TPU:0, one launch (start us, length us, event | category | flops | bytes accessed | tf_op | source)
XLA Modules:
  0.0 542.7 jit_solution(3535838593089581746)
XLA Ops:
  12.7 4.7 collective-permute-start.7
  21.6 25.2 %collective-permute-done.1 = bf16[5,512]{1,0:T(8,128)(2,1)S(1)} collective-permute-done((bf16[5,512]{1,0:T(8,128)(2,1)S(1)}, bf16[5,512]{1,0:T(8,128)(2,1)S(1)}, u32[]{:S(2)}, u32[]{:S(2)}) %collective-permute-start.1) | collective-permute-done | bytes 5152 | tf_op jit(solution)/shard_map/ppermute | solution.py:24
  63.7 5.4 fusion.73
  73.1 4.2 convolution_convert_fusion.4
  79.7 23.4 %collective-permute-done.17 = bf16[512,1024]{1,0:T(8,128)(2,1)} collective-permute-done((bf16[512,1024]{1,0:T(8,128)(2,1)}, bf16[512,1024]{1,0:T(8,128)(2,1)}, u32[]{:S(2)}, u32[]{:S(2)}) %collective-permute-start.17) | collective-permute-done | bytes 1048608 | tf_op jit(solution)/shard_map/ppermute | solution.py:24
  113.5 4.5 fusion.61
  118.0 4.5 fusion.69
  122.5 9.8 %multiply_convert_fusion.2 = (bf16[1024,1152]{1,0:T(8,128)(2,1)S(1)}, bf16[1024,1152]{1,0:T(8,128)(2,1)}, bf16[1024,1152]{1,0:T(8,128)(2,1)}) fusion(f32[1024,1152]{1,0:T(8,128)} %fusion.69, f32[1024,1152]{1,0:T(8,128)} %fusion.61, bf16[2304,1024]{1,0:T(8,128)(2,1)S(1)} %bitcast.220, s32[]{:T(128)S(6)} %select_n.227, ...), kind=kOutput, calls=%fused_computation.14 | convolution fusion | flops 2437808128 | bytes 20971524 | tf_op jit(solution)/shard_map/dot_general | solution.py:40
  132.3 6.1 %fusion.65 = f32[1024,1024]{1,0:T(8,128)S(1)} fusion(bf16[1024,1152]{1,0:T(8,128)(2,1)} %get-tuple-element.24, bf16[1024,2304]{1,0:T(8,128)(2,1)} %param.16, s32[]{:T(128)S(6)} %select_n.227), kind=kOutput, calls=%fused_computation.113 | convolution fusion | flops 2415919104 | bytes 8912900 | tf_op jit(solution)/shard_map/dot_general | solution.py:40
  138.8 5.0 add_convert_fusion.1
  149.7 4.5 fusion.59
  154.1 4.5 fusion.67
  158.6 11.5 %multiply_convert_fusion = (bf16[1024,1152]{1,0:T(8,128)(2,1)S(1)}, bf16[1024,1152]{1,0:T(8,128)(2,1)}, bf16[1024,1152]{1,0:T(8,128)(2,1)}) fusion(f32[1024,1152]{1,0:T(8,128)} %fusion.67, f32[1024,1152]{1,0:T(8,128)} %fusion.59, bf16[2304,1024]{1,0:T(8,128)(2,1)} %param.18, s32[]{:T(128)S(6)} %select_n.227, bf16[512,1024]{1,0:T(8,128)(2,1)} %collective-permute-done.18, ...), kind=kOutput, calls=%fused_computation.12 | convolution fusion | flops 2437808128 | bytes 20971524 | tf_op jit(solution)/shard_map/dot_general | solution.py:40
  170.1 6.1 %convolution_convert_fusion.1 = bf16[1024,1024]{1,0:T(8,128)(2,1)S(1)} fusion(bf16[1024,1152]{1,0:T(8,128)(2,1)} %get-tuple-element.28, bf16[2304,1024]{1,0:T(8,128)(2,1)} %param.18, s32[]{:T(128)S(6)} %select_n.227), kind=kOutput, calls=%fused_computation.96 | convolution fusion | flops 2416967680 | bytes 6815748 | tf_op jit(solution)/shard_map/dot_general | solution.py:32
  177.6 4.6 fusion.63
  187.7 9.3 %fusion.21 = bf16[1024,1152]{1,0:T(8,128)(2,1)S(1)} fusion(bf16[1024,1152]{1,0:T(8,128)(2,1)} %get-tuple-element.28, bf16[1024,1152]{1,0:T(8,128)(2,1)} %get-tuple-element.25, bf16[512,1024]{1,0:T(8,128)(2,1)} %collective-permute-done.18, bf16[512,1024]{1,0:T(8,128)(2,1)} %collective-permute-done.17, bf16[512,1024]{1,0:T(8,128)(2,1)} %collective-permute-done.15, ...), kind=kOutput, calls=%fused_computation.37 | convolution fusion | flops 4859232256 | bytes 11272192 | tf_op jit(solution)/shard_map/dot_general | solution.py:36
  199.9 8.2 %fusion.26 = bf16[1024,1152]{1,0:T(8,128)(2,1)S(1)} fusion(bf16[1024,1152]{1,0:T(8,128)(2,1)} %copy-done.38, bf16[1024,1152]{1,0:T(8,128)(2,1)} %copy-done.37, bf16[512,1024]{1,0:T(8,128)(2,1)S(1)} %collective-permute-done.12, bf16[512,1024]{1,0:T(8,128)(2,1)S(1)} %collective-permute-done.11, bf16[1024,1024]{1,0:T(8,128)(2,1)S(1)} %multiply_convert_fusion.6), kind=kOutput, calls=%fused_computation.38 | convolution fusion | flops 4855037952 | bytes 11272192 | tf_op jit(solution)/shard_map/dot_general | solution.py:36
  210.2 8.8 %fusion.29 = bf16[1024,1152]{1,0:T(8,128)(2,1)S(1)} fusion(bf16[1024,1152]{1,0:T(8,128)(2,1)} %get-tuple-element.27, bf16[1024,1152]{1,0:T(8,128)(2,1)} %get-tuple-element.24, bf16[512,1024]{1,0:T(8,128)(2,1)} %copy-done.24, bf16[512,1024]{1,0:T(8,128)(2,1)} %copy-done.23, bf16[1024,1024]{1,0:T(8,128)(2,1)S(1)} %multiply_convert_fusion.6), kind=kOutput, calls=%fused_computation.39 | convolution fusion | flops 4855037952 | bytes 11272192 | tf_op jit(solution)/shard_map/dot_general | solution.py:36
  229.3 23.5 %collective-permute-done.34 = bf16[4,128,1152]{2,1,0:T(8,128)(2,1)} collective-permute-done((bf16[4,128,1152]{2,1,0:T(8,128)(2,1)}, bf16[4,128,1152]{2,1,0:T(8,128)(2,1)}, u32[]{:S(2)}, u32[]{:S(2)}) %collective-permute-start.34) | collective-permute-done | bytes 1179680 | tf_op jit(solution)/shard_map/ppermute | solution.py:12
  255.6 21.7 %collective-permute-done.30 = bf16[4,128,1152]{2,1,0:T(8,128)(2,1)S(1)} collective-permute-done((bf16[4,128,1152]{2,1,0:T(8,128)(2,1)S(1)}, bf16[4,128,1152]{2,1,0:T(8,128)(2,1)S(1)}, u32[]{:S(2)}, u32[]{:S(2)}) %collective-permute-start.30) | collective-permute-done | bytes 1179680 | tf_op jit(solution)/shard_map/ppermute | solution.py:12
  280.6 12.9 %collective-permute-done.35 = bf16[2,128,1152]{2,1,0:T(8,128)(2,1)S(1)} collective-permute-done((bf16[2,128,1152]{2,1,0:T(8,128)(2,1)S(1)}, bf16[2,128,1152]{2,1,0:T(8,128)(2,1)S(1)}, u32[]{:S(2)}, u32[]{:S(2)}) %collective-permute-start.35) | collective-permute-done | bytes 589856 | tf_op jit(solution)/shard_map/ppermute | solution.py:12
  295.2 9.4 %collective-permute-done.31 = bf16[2,128,1152]{2,1,0:T(8,128)(2,1)S(1)} collective-permute-done((bf16[2,128,1152]{2,1,0:T(8,128)(2,1)S(1)}, bf16[2,128,1152]{2,1,0:T(8,128)(2,1)S(1)}, u32[]{:S(2)}, u32[]{:S(2)}) %collective-permute-start.31) | collective-permute-done | bytes 589856 | tf_op jit(solution)/shard_map/ppermute | solution.py:12
  307.3 11.9 %collective-permute-done.40 = bf16[1,128,1152]{2,1,0:T(8,128)(2,1)S(1)} collective-permute-done((bf16[1,128,1152]{2,1,0:T(8,128)(2,1)S(1)}, bf16[1,128,1152]{2,1,0:T(8,128)(2,1)S(1)}, u32[]{:S(2)}, u32[]{:S(2)}) %collective-permute-start.40) | collective-permute-done | bytes 294944 | tf_op jit(solution)/shard_map/ppermute | solution.py:12
  320.3 13.9 %collective-permute-done.36 = bf16[1,128,1152]{2,1,0:T(8,128)(2,1)S(1)} collective-permute-done((bf16[1,128,1152]{2,1,0:T(8,128)(2,1)S(1)}, bf16[1,128,1152]{2,1,0:T(8,128)(2,1)S(1)}, u32[]{:S(2)}, u32[]{:S(2)}) %collective-permute-start.36) | collective-permute-done | bytes 294944 | tf_op jit(solution)/shard_map/ppermute | solution.py:12
  336.8 11.6 %collective-permute-done.32 = bf16[1,128,1152]{2,1,0:T(8,128)(2,1)S(1)} collective-permute-done((bf16[1,128,1152]{2,1,0:T(8,128)(2,1)S(1)}, bf16[1,128,1152]{2,1,0:T(8,128)(2,1)S(1)}, u32[]{:S(2)}, u32[]{:S(2)}) %collective-permute-start.32) | collective-permute-done | bytes 294944 | tf_op jit(solution)/shard_map/ppermute | solution.py:12
  349.5 4.0 fusion.122
  366.2 4.6 multiply_reduce_fusion.6
  389.8 40.1 %collective-permute-done.25 = bf16[8,128,1024]{2,1,0:T(8,128)(2,1)S(1)} collective-permute-done((bf16[8,128,1024]{2,1,0:T(8,128)(2,1)S(1)}, bf16[8,128,1024]{2,1,0:T(8,128)(2,1)S(1)}, u32[]{:S(2)}, u32[]{:S(2)}) %collective-permute-start.25) | collective-permute-done | bytes 2097184 | tf_op jit(solution)/shard_map/ppermute | solution.py:24
  435.1 21.7 %collective-permute-done.26 = bf16[4,128,1024]{2,1,0:T(8,128)(2,1)S(1)} collective-permute-done((bf16[4,128,1024]{2,1,0:T(8,128)(2,1)S(1)}, bf16[4,128,1024]{2,1,0:T(8,128)(2,1)S(1)}, u32[]{:S(2)}, u32[]{:S(2)}) %collective-permute-start.26) | collective-permute-done | bytes 1048608 | tf_op jit(solution)/shard_map/ppermute | solution.py:12
  459.2 11.3 %collective-permute-done.27 = bf16[2,128,1024]{2,1,0:T(8,128)(2,1)S(1)} collective-permute-done((bf16[2,128,1024]{2,1,0:T(8,128)(2,1)S(1)}, bf16[2,128,1024]{2,1,0:T(8,128)(2,1)S(1)}, u32[]{:S(2)}, u32[]{:S(2)}) %collective-permute-start.27) | collective-permute-done | bytes 524320 | tf_op jit(solution)/shard_map/ppermute | solution.py:12
  471.4 7.6 %psum.14 = f32[5,1024]{1,0:T(8,128)S(1)} all-reduce(f32[5,1024]{1,0:T(8,128)S(1)} %pad_maximum_fusion.23), channel_id=1, replica_groups=mesh['seq'=16,'wshard'=2] {'wshard'}, use_global_device_ids=true, to_apply=%region_10.11 | all-reduce | flops 5120 | bytes 40960 | tf_op jit(solution)/shard_map/psum | solution.py:347
  479.0 57.6 %psum.15 = f32[5,1024]{1,0:T(8,128)S(1)} all-reduce(f32[5,1024]{1,0:T(8,128)S(1)} %psum.14), channel_id=1, replica_groups=mesh['seq'=16,'wshard'=2] {'seq'}, use_global_device_ids=true, to_apply=%region_11.12 | all-reduce | flops 5120 | bytes 40960 | tf_op jit(solution)/shard_map/psum | solution.py:350
  (343 shorter events, 138.5 us)
Async XLA Ops:
  5.7 41.8 %collective-permute-start.5 = (bf16[4,2,1152]{2,0,1:T(4,128)(2,1)S(1)}, bf16[4,2,1152]{2,0,1:T(4,128)(2,1)S(1)}, u32[]{:S(2)}, u32[]{:S(2)}) collective-permute-start(bf16[4,2,1152]{2,0,1:T(4,128)(2,1)S(1)} %get-tuple-element.69), channel_id=1, source_target_pairs={{4,0},{8,4},{12,8},{16,12},{20,16},{24,20},{28,24},{5,1},{9,5},{13... | collective-permute-start | bytes 55304 | tf_op jit(solution)/shard_map/ppermute | solution.py:12
  7.0 41.0 %collective-permute-start.6 = (bf16[4,2,1152]{2,0,1:T(4,128)(2,1)S(1)}, bf16[4,2,1152]{2,0,1:T(4,128)(2,1)S(1)}, u32[]{:S(2)}, u32[]{:S(2)}) collective-permute-start(bf16[4,2,1152]{2,0,1:T(4,128)(2,1)S(1)} %get-tuple-element.69), channel_id=1, source_target_pairs={{4,2},{8,6},{12,10},{16,14},{20,18},{24,22},{28,26},{5,3},{9,7},{1... | collective-permute-start | bytes 55304 | tf_op jit(solution)/shard_map/ppermute | solution.py:12
  9.0 42.0 %collective-permute-start.2 = (bf16[3,1024,256]{2,1,0:T(8,128)(2,1)}, bf16[3,1024,256]{2,1,0:T(8,128)(2,1)}, u32[]{:S(2)}, u32[]{:S(2)}) collective-permute-start(bf16[3,1024,256]{2,1,0:T(8,128)(2,1)} %dynamic-slice_bitcast_fusion), channel_id=1, source_target_pairs={{0,1},{1,0},{2,3},{3,2},{4,5},{5,4},{6,7},{7,6},{8,9},{9,8},{10,11... | collective-permute-start | bytes 4718600 | tf_op jit(solution)/shard_map/ppermute | solution.py:24
  11.9 37.5 %collective-permute-start.3 = (bf16[4,2,1152]{2,0,1:T(4,128)(2,1)S(1)}, bf16[4,2,1152]{2,0,1:T(4,128)(2,1)S(1)}, u32[]{:S(2)}, u32[]{:S(2)}) collective-permute-start(bf16[4,2,1152]{2,0,1:T(4,128)(2,1)S(1)} %get-tuple-element.68), channel_id=1, source_target_pairs={{2,4},{6,8},{10,12},{14,16},{18,20},{22,24},{26,28},{3,5},{7,9},{1... | collective-permute-start | bytes 55304 | tf_op jit(solution)/shard_map/ppermute | solution.py:12
  21.3 25.4 %collective-permute-start.1 = (bf16[5,512]{1,0:T(8,128)(2,1)S(1)}, bf16[5,512]{1,0:T(8,128)(2,1)S(1)}, u32[]{:S(2)}, u32[]{:S(2)}) collective-permute-start(bf16[5,512]{1,0:T(8,128)(2,1)S(1)} %pad_maximum_fusion.26), channel_id=1, source_target_pairs={{0,1},{1,0},{2,3},{3,2},{4,5},{5,4},{6,7},{7,6},{8,9},{9,8},{10,11... | collective-permute-start | bytes 15368 | tf_op jit(solution)/shard_map/ppermute | solution.py:24
  48.0 25.1 %collective-permute-start.8 = (bf16[256,1024]{1,0:T(8,128)(2,1)}, bf16[256,1024]{1,0:T(8,128)(2,1)}, u32[]{:S(2)}, u32[]{:S(2)}) collective-permute-start(bf16[256,1024]{1,0:T(8,128)(2,1)} %constant_dynamic-slice_fusion.25), channel_id=1, source_target_pairs={{0,1},{1,0},{2,3},{3,2},{4,5},{5,4},{6,7},{7,6},{8,9},{9,8},{10,11... | collective-permute-start | bytes 1572872 | tf_op jit(solution)/shard_map/ppermute | solution.py:24
  77.2 29.5 %collective-permute-start.9 = (bf16[1024,1024]{1,0:T(8,128)(2,1)}, bf16[1024,1024]{1,0:T(8,128)(2,1)}, u32[]{:S(2)}, u32[]{:S(2)}) collective-permute-start(bf16[1024,1024]{1,0:T(8,128)(2,1)} %convolution_convert_fusion.4), channel_id=1, source_target_pairs={{0,2},{2,0},{4,6},{6,4},{8,10},{10,8},{12,14},{14,12},{16,18},{18,... | collective-permute-start | bytes 6291464 | tf_op jit(solution)/shard_map/ppermute | solution.py:12
  77.4 25.7 %collective-permute-start.17 = (bf16[512,1024]{1,0:T(8,128)(2,1)}, bf16[512,1024]{1,0:T(8,128)(2,1)}, u32[]{:S(2)}, u32[]{:S(2)}) collective-permute-start(bf16[512,1024]{1,0:T(8,128)(2,1)} %bitcast.18), channel_id=1, source_target_pairs={{0,1},{1,0},{2,3},{3,2},{4,5},{5,4},{6,7},{7,6},{8,9},{9,8},{10,11... | collective-permute-start | bytes 3145736 | tf_op jit(solution)/shard_map/ppermute | solution.py:24
  78.9 43.6 %collective-permute-start.15 = (bf16[512,1024]{1,0:T(8,128)(2,1)}, bf16[512,1024]{1,0:T(8,128)(2,1)}, u32[]{:S(2)}, u32[]{:S(2)}) collective-permute-start(bf16[512,1024]{1,0:T(8,128)(2,1)} %bitcast.18), channel_id=1, source_target_pairs={{0,2},{2,0},{4,6},{6,4},{8,10},{10,8},{12,14},{14,12},{16,18},{18,... | collective-permute-start | bytes 3145736 | tf_op jit(solution)/shard_map/ppermute | solution.py:12
  103.1 55.5 %collective-permute-start.18 = (bf16[512,1024]{1,0:T(8,128)(2,1)}, bf16[512,1024]{1,0:T(8,128)(2,1)}, u32[]{:S(2)}, u32[]{:S(2)}) collective-permute-start(bf16[512,1024]{1,0:T(8,128)(2,1)} %collective-permute-done.17), channel_id=1, source_target_pairs={{0,2},{2,0},{4,6},{6,4},{8,10},{10,8},{12,14},{14,12},{16,18},{18,... | collective-permute-start | bytes 3145736 | tf_op jit(solution)/shard_map/ppermute | solution.py:12
  111.9 26.6 %collective-permute-start.11 = (bf16[512,1024]{1,0:T(8,128)(2,1)S(1)}, bf16[512,1024]{1,0:T(8,128)(2,1)S(1)}, u32[]{:S(2)}, u32[]{:S(2)}) collective-permute-start(bf16[512,1024]{1,0:T(8,128)(2,1)S(1)} %slice.503), channel_id=1, source_target_pairs={{0,1},{1,0},{2,3},{3,2},{4,5},{5,4},{6,7},{7,6},{8,9},{9,8},{10,11... | collective-permute-start | bytes 3145736 | tf_op jit(solution)/shard_map/ppermute | solution.py:24
  144.8 203.7 %collective-permute-start.16 = (bf16[512,1024]{1,0:T(8,128)(2,1)}, bf16[512,1024]{1,0:T(8,128)(2,1)S(1)}, u32[]{:S(2)}, u32[]{:S(2)}) collective-permute-start(bf16[512,1024]{1,0:T(8,128)(2,1)} %slice.507), channel_id=1, source_target_pairs={{0,2},{2,0},{4,6},{6,4},{8,10},{10,8},{12,14},{14,12},{16,18},{18,... | collective-permute-start | bytes 3145736 | tf_op jit(solution)/shard_map/ppermute | solution.py:12
  177.3 42.1 %collective-permute-start.13 = (bf16[512,1024]{1,0:T(8,128)(2,1)}, bf16[512,1024]{1,0:T(8,128)(2,1)}, u32[]{:S(2)}, u32[]{:S(2)}) collective-permute-start(bf16[512,1024]{1,0:T(8,128)(2,1)} %slice.505), channel_id=1, source_target_pairs={{0,2},{2,0},{4,6},{6,4},{8,10},{10,8},{12,14},{14,12},{16,18},{18,... | collective-permute-start | bytes 3145736 | tf_op jit(solution)/shard_map/ppermute | solution.py:12
  187.4 35.1 %collective-permute-start.19 = (bf16[512,1024]{1,0:T(8,128)(2,1)}, bf16[512,1024]{1,0:T(8,128)(2,1)}, u32[]{:S(2)}, u32[]{:S(2)}) collective-permute-start(bf16[512,1024]{1,0:T(8,128)(2,1)} %slice.509), channel_id=1, source_target_pairs={{0,2},{2,0},{4,6},{6,4},{8,10},{10,8},{12,14},{14,12},{16,18},{18,... | collective-permute-start | bytes 3145736 | tf_op jit(solution)/shard_map/ppermute | solution.py:12
  198.4 29.1 %collective-permute-start.38 = (bf16[4,128,1152]{2,1,0:T(8,128)(2,1)}, bf16[4,128,1152]{2,1,0:T(8,128)(2,1)}, u32[]{:S(2)}, u32[]{:S(2)}) collective-permute-start(bf16[4,128,1152]{2,1,0:T(8,128)(2,1)} %pad_maximum_fusion.16), channel_id=1, source_target_pairs={{0,4},{2,6},{4,0},{6,2},{8,12},{10,14},{12,8},{14,10},{16,20},{18,... | collective-permute-start | bytes 3538952 | tf_op jit(solution)/shard_map/ppermute | solution.py:12
  209.7 43.1 %collective-permute-start.34 = (bf16[4,128,1152]{2,1,0:T(8,128)(2,1)}, bf16[4,128,1152]{2,1,0:T(8,128)(2,1)}, u32[]{:S(2)}, u32[]{:S(2)}) collective-permute-start(bf16[4,128,1152]{2,1,0:T(8,128)(2,1)} %pad_maximum_fusion.15), channel_id=1, source_target_pairs={{0,4},{2,6},{4,0},{6,2},{8,12},{10,14},{12,8},{14,10},{16,20},{18,... | collective-permute-start | bytes 3538952 | tf_op jit(solution)/shard_map/ppermute | solution.py:12
  220.2 129.3 %collective-permute-start.10 = (bf16[512,1024]{1,0:T(8,128)(2,1)S(1)}, bf16[512,1024]{1,0:T(8,128)(2,1)S(1)}, u32[]{:S(2)}, u32[]{:S(2)}) collective-permute-start(bf16[512,1024]{1,0:T(8,128)(2,1)S(1)} %copy-done.22), channel_id=1, source_target_pairs={{0,2},{2,0},{4,6},{6,4},{8,10},{10,8},{12,14},{14,12},{16,18},{18,... | collective-permute-start | bytes 3145736 | tf_op jit(solution)/shard_map/ppermute | solution.py:12
  222.5 54.7 %collective-permute-start.30 = (bf16[4,128,1152]{2,1,0:T(8,128)(2,1)S(1)}, bf16[4,128,1152]{2,1,0:T(8,128)(2,1)S(1)}, u32[]{:S(2)}, u32[]{:S(2)}) collective-permute-start(bf16[4,128,1152]{2,1,0:T(8,128)(2,1)S(1)} %pad_maximum_fusion.14), channel_id=1, source_target_pairs={{0,4},{2,6},{4,0},{6,2},{8,12},{10,14},{12,8},{14,10},{16,20},{18,... | collective-permute-start | bytes 3538952 | tf_op jit(solution)/shard_map/ppermute | solution.py:12
  227.5 122.0 %collective-permute-start.14 = (bf16[512,1024]{1,0:T(8,128)(2,1)S(1)}, bf16[512,1024]{1,0:T(8,128)(2,1)S(1)}, u32[]{:S(2)}, u32[]{:S(2)}) collective-permute-start(bf16[512,1024]{1,0:T(8,128)(2,1)S(1)} %add_convert_fusion.5), channel_id=1, source_target_pairs={{0,1},{1,0},{2,3},{3,2},{4,5},{5,4},{6,7},{7,6},{8,9},{9,8},{10,11... | collective-permute-start | bytes 3145736 | tf_op jit(solution)/shard_map/ppermute | solution.py:24
  252.8 26.2 %collective-permute-start.39 = (bf16[2,128,1152]{2,1,0:T(8,128)(2,1)S(1)}, bf16[2,128,1152]{2,1,0:T(8,128)(2,1)S(1)}, u32[]{:S(2)}, u32[]{:S(2)}) collective-permute-start(bf16[2,128,1152]{2,1,0:T(8,128)(2,1)S(1)} %add_convert_fusion.6), channel_id=1, source_target_pairs={{0,8},{2,10},{4,12},{6,14},{8,0},{10,2},{12,4},{14,6},{16,24},{18,... | collective-permute-start | bytes 1769480 | tf_op jit(solution)/shard_map/ppermute | solution.py:12
  277.3 16.3 %collective-permute-start.35 = (bf16[2,128,1152]{2,1,0:T(8,128)(2,1)S(1)}, bf16[2,128,1152]{2,1,0:T(8,128)(2,1)S(1)}, u32[]{:S(2)}, u32[]{:S(2)}) collective-permute-start(bf16[2,128,1152]{2,1,0:T(8,128)(2,1)S(1)} %add_convert_fusion.7), channel_id=1, source_target_pairs={{0,8},{2,10},{4,12},{6,14},{8,0},{10,2},{12,4},{14,6},{16,24},{18,... | collective-permute-start | bytes 1769480 | tf_op jit(solution)/shard_map/ppermute | solution.py:12
  279.0 25.6 %collective-permute-start.31 = (bf16[2,128,1152]{2,1,0:T(8,128)(2,1)S(1)}, bf16[2,128,1152]{2,1,0:T(8,128)(2,1)S(1)}, u32[]{:S(2)}, u32[]{:S(2)}) collective-permute-start(bf16[2,128,1152]{2,1,0:T(8,128)(2,1)S(1)} %add_convert_fusion.8), channel_id=1, source_target_pairs={{0,8},{2,10},{4,12},{6,14},{8,0},{10,2},{12,4},{14,6},{16,24},{18,... | collective-permute-start | bytes 1769480 | tf_op jit(solution)/shard_map/ppermute | solution.py:12
  293.5 55.0 %collective-permute-start.20 = (bf16[512,1024]{1,0:T(8,128)(2,1)S(1)}, bf16[512,1024]{1,0:T(8,128)(2,1)S(1)}, u32[]{:S(2)}, u32[]{:S(2)}) collective-permute-start(bf16[512,1024]{1,0:T(8,128)(2,1)S(1)} %add_convert_fusion.3), channel_id=1, source_target_pairs={{0,1},{1,0},{2,3},{3,2},{4,5},{5,4},{6,7},{7,6},{8,9},{9,8},{10,11... | collective-permute-start | bytes 3145736 | tf_op jit(solution)/shard_map/ppermute | solution.py:24
  304.6 14.6 %collective-permute-start.40 = (bf16[1,128,1152]{2,1,0:T(8,128)(2,1)S(1)}, bf16[1,128,1152]{2,1,0:T(8,128)(2,1)S(1)}, u32[]{:S(2)}, u32[]{:S(2)}) collective-permute-start(bf16[1,128,1152]{2,1,0:T(8,128)(2,1)S(1)} %add_convert_fusion.10), channel_id=1, source_target_pairs={{0,16},{2,18},{4,20},{6,22},{8,24},{10,26},{12,28},{14,30},{16,0},... | collective-permute-start | bytes 884744 | tf_op jit(solution)/shard_map/ppermute | solution.py:12
  319.2 15.0 %collective-permute-start.36 = (bf16[1,128,1152]{2,1,0:T(8,128)(2,1)S(1)}, bf16[1,128,1152]{2,1,0:T(8,128)(2,1)S(1)}, u32[]{:S(2)}, u32[]{:S(2)}) collective-permute-start(bf16[1,128,1152]{2,1,0:T(8,128)(2,1)S(1)} %add_convert_fusion.11), channel_id=1, source_target_pairs={{0,16},{2,18},{4,20},{6,22},{8,24},{10,26},{12,28},{14,30},{16,0},... | collective-permute-start | bytes 884744 | tf_op jit(solution)/shard_map/ppermute | solution.py:12
  334.3 14.1 %collective-permute-start.32 = (bf16[1,128,1152]{2,1,0:T(8,128)(2,1)S(1)}, bf16[1,128,1152]{2,1,0:T(8,128)(2,1)S(1)}, u32[]{:S(2)}, u32[]{:S(2)}) collective-permute-start(bf16[1,128,1152]{2,1,0:T(8,128)(2,1)S(1)} %add_convert_fusion.12), channel_id=1, source_target_pairs={{0,16},{2,18},{4,20},{6,22},{8,24},{10,26},{12,28},{14,30},{16,0},... | collective-permute-start | bytes 884744 | tf_op jit(solution)/shard_map/ppermute | solution.py:12
  353.5 12.7 %collective-permute-start.21 = (bf16[512,1024]{1,0:T(8,128)(2,1)}, bf16[512,1024]{1,0:T(8,128)(2,1)}, u32[]{:S(2)}, u32[]{:S(2)}) collective-permute-start(bf16[512,1024]{1,0:T(8,128)(2,1)} %get-tuple-element.19), channel_id=1, source_target_pairs={{0,2},{2,0},{4,6},{6,4},{8,10},{10,8},{12,14},{14,12},{16,18},{18,... | collective-permute-start | bytes 3145736 | tf_op jit(solution)/shard_map/ppermute | solution.py:12
  381.4 48.4 %collective-permute-start.25 = (bf16[8,128,1024]{2,1,0:T(8,128)(2,1)S(1)}, bf16[8,128,1024]{2,1,0:T(8,128)(2,1)S(1)}, u32[]{:S(2)}, u32[]{:S(2)}) collective-permute-start(bf16[8,128,1024]{2,1,0:T(8,128)(2,1)S(1)} %dynamic-slice_dynamic-update-slice_fusion), channel_id=1, source_target_pairs={{0,1},{1,0},{2,3},{3,2},{4,5},{5,4},{6,7},{7,6},{8,9},{9,8},{10,11... | collective-permute-start | bytes 6291464 | tf_op jit(solution)/shard_map/ppermute | solution.py:24
  388.5 45.8 %collective-permute-start.24 = (bf16[512,1024]{1,0:T(8,128)(2,1)S(1)}, bf16[512,1024]{1,0:T(8,128)(2,1)S(1)}, u32[]{:S(2)}, u32[]{:S(2)}) collective-permute-start(bf16[512,1024]{1,0:T(8,128)(2,1)S(1)} %slice.522), channel_id=1, source_target_pairs={{0,2},{2,0},{4,6},{6,4},{8,10},{10,8},{12,14},{14,12},{16,18},{18,... | collective-permute-start | bytes 3145736 | tf_op jit(solution)/shard_map/ppermute | solution.py:12
  430.3 26.4 %collective-permute-start.26 = (bf16[4,128,1024]{2,1,0:T(8,128)(2,1)S(1)}, bf16[4,128,1024]{2,1,0:T(8,128)(2,1)S(1)}, u32[]{:S(2)}, u32[]{:S(2)}) collective-permute-start(bf16[4,128,1024]{2,1,0:T(8,128)(2,1)S(1)} %add_convert_fusion.2), channel_id=1, source_target_pairs={{0,4},{2,6},{4,0},{6,2},{8,12},{10,14},{12,8},{14,10},{16,20},{18,... | collective-permute-start | bytes 3145736 | tf_op jit(solution)/shard_map/ppermute | solution.py:12
  457.0 13.5 %collective-permute-start.27 = (bf16[2,128,1024]{2,1,0:T(8,128)(2,1)S(1)}, bf16[2,128,1024]{2,1,0:T(8,128)(2,1)S(1)}, u32[]{:S(2)}, u32[]{:S(2)}) collective-permute-start(bf16[2,128,1024]{2,1,0:T(8,128)(2,1)S(1)} %add_convert_fusion.9), channel_id=1, source_target_pairs={{0,8},{2,10},{4,12},{6,14},{8,0},{10,2},{12,4},{14,6},{16,24},{18,... | collective-permute-start | bytes 1572872 | tf_op jit(solution)/shard_map/ppermute | solution.py:12
  471.3 66.6 %collective-permute-start.28 = (bf16[1,128,1024]{2,1,0:T(8,128)(2,1)S(1)}, bf16[1,128,1024]{2,1,0:T(8,128)(2,1)S(1)}, u32[]{:S(2)}, u32[]{:S(2)}) collective-permute-start(bf16[1,128,1024]{2,1,0:T(8,128)(2,1)S(1)} %add_convert_fusion.13), channel_id=1, source_target_pairs={{0,16},{2,18},{4,20},{6,22},{8,24},{10,26},{12,28},{14,30},{16,0},... | collective-permute-start | bytes 786440 | tf_op jit(solution)/shard_map/ppermute | solution.py:12
  (65 other events, 660.6 us)
